TPU v7x, 128 devices: a whole 4x4x4 slice. The times are simulated.
128 devices in a mesh: section: 2 (over z_lo), chan: 8 (over x, z_hi), batch: 8 (over y, core).
Axes of the slice: x: 4, y: 4, z: 4 (z_hi: 2, z_lo: 2; z = z_hi * 2 + z_lo), core: 2. Of those that a mesh axis runs over, the one named last changes fastest.
Arguments:
- images: bfloat16 [2, 8, 8, 256, 1024], P('section', 'batch', 'chan'), may hold values from -12 to 12
- w_early: bfloat16 [1024, 2048], replicated, may hold values from -0.1875 to 0.1875
- gain_early: float32 [2048], replicated, may hold values from 0.5 to 1.5
- bias_early: float32 [2048], replicated, may hold values from -0.5 to 0.5
- w_late: bfloat16 [2048, 8192], P(None, 'chan'), may hold values from -0.125 to 0.125
- gain_late: float32 [8192], P('chan'), may hold values from 0.5 to 1.5
- bias_late: float32 [8192], P('chan'), may hold values from -0.5 to 0.5
- cotangent: bfloat16 [2, 64, 256, 8192], P('section', 'batch', None, 'chan'), may hold values from -6 to 6
Outputs:
- late_out: bfloat16 [2, 64, 256, 8192], P('section', 'batch', None, 'chan')
- grad_late: float32 [2048, 8192], P(None, 'chan')
- grad_early: float32 [1024, 2048], P(('section', 'chan', 'batch'))
All inputs are finite; a program needn't handle non-finite values.
Results may differ from a plain program's by a relative error of at most 0.024.
Values may be sent and summed in bfloat16 or wider, within the bound.
No kernel may reach another device: no remote copies, remote signals or barrier semaphores. Data moves between devices by JAX's collectives and lax.ppermute only.
A program may use at most 192 MiB of HBM per device.

v0:
```python
import jax
import jax.numpy as jnp
from jax import lax
from jax.sharding import PartitionSpec as P


def smooth_gate(values):
    return values * jax.nn.sigmoid(values)


def smooth_slope(values):
    sig = jax.nn.sigmoid(values)
    return sig * (1.0 + values * (1.0 - sig))


def body(images, w_early, gain_early, bias_early, w_late, gain_late, bias_late, cotangent):
    micro, batch_one, img_dev, pixels, width_in = images.shape
    width_mid = w_early.shape[1]
    width_out = w_late.shape[1]
    chan_count = lax.axis_size("chan")
    batch_count = lax.axis_size("batch")
    flat_in = images.reshape(-1, width_in)
    early_raw = jnp.dot(flat_in, w_early, preferred_element_type=jnp.float32).astype(jnp.bfloat16)
    total_rows = flat_in.shape[0] * chan_count * batch_count
    raw_f = early_raw.astype(jnp.float32)
    sum_one, sum_two = lax.psum((jnp.sum(raw_f, 0), jnp.sum(raw_f * raw_f, 0)), ("chan", "batch"))
    mean_e = sum_one / total_rows
    rstd_e = lax.rsqrt(sum_two / total_rows - mean_e * mean_e + 1e-05)
    normed_e = (raw_f - mean_e) * rstd_e
    pre_e = normed_e * gain_early + bias_early
    act_local = smooth_gate(pre_e).astype(jnp.bfloat16).reshape(img_dev, pixels, width_mid)
    act_full = lax.all_gather(act_local, "chan", axis=0, tiled=True)
    act_rows = act_full.reshape(-1, width_mid)
    late = jnp.dot(act_rows, w_late, preferred_element_type=jnp.float32)
    late_rows = act_rows.shape[0] * batch_count
    late_one, late_two = lax.psum((jnp.sum(late, 0), jnp.sum(late * late, 0)), "batch")
    mean_l = late_one / late_rows
    rstd_l = lax.rsqrt(late_two / late_rows - mean_l * mean_l + 1e-05)
    normed_l = (late - mean_l) * rstd_l
    pre_l = normed_l * gain_late + bias_late
    late_out = smooth_gate(pre_l).astype(jnp.bfloat16).reshape(cotangent.shape)
    grad_y = cotangent.reshape(-1, width_out).astype(jnp.float32) * smooth_slope(pre_l)
    back_one, back_two = lax.psum((jnp.sum(grad_y, 0), jnp.sum(grad_y * normed_l, 0)), "batch")
    grad_h = (
        gain_late * rstd_l * (grad_y - back_one / late_rows - normed_l * (back_two / late_rows))
    ).astype(jnp.bfloat16)
    local_late = lax.dot_general(
        act_rows, grad_h, (((0,), (0,)), ((), ())), preferred_element_type=jnp.float32
    )
    grad_late = lax.psum(local_late.astype(jnp.bfloat16), ("section", "batch")).astype(jnp.float32)
    grad_cube = grad_h.reshape(-1, pixels, width_out)
    piece = grad_cube
    grad_act = lax.psum_scatter(
        jnp.einsum("ipl,al->ipa", piece, w_late, preferred_element_type=jnp.float32).astype(
            jnp.bfloat16
        ),
        "chan",
        scatter_dimension=0,
        tiled=True,
    ).astype(jnp.float32)
    grad_act = grad_act.reshape(-1, width_mid)
    grad_pre = grad_act * smooth_slope(pre_e)
    early_one, early_two = lax.psum(
        (jnp.sum(grad_pre, 0), jnp.sum(grad_pre * normed_e, 0)), ("chan", "batch")
    )
    grad_raw = (
        gain_early
        * rstd_e
        * (grad_pre - early_one / total_rows - normed_e * (early_two / total_rows))
    ).astype(jnp.bfloat16)
    piece = flat_in
    grad_early = lax.psum_scatter(
        lax.dot_general(
            piece, grad_raw, (((0,), (0,)), ((), ())), preferred_element_type=jnp.float32
        ),
        ("section", "chan", "batch"),
        scatter_dimension=0,
        tiled=True,
    )
    return (late_out, grad_late, grad_early)


def solution(mesh):
    return jax.shard_map(
        body,
        mesh=mesh,
        in_specs=(
            P("section", "batch", "chan", None, None),
            P(),
            P(),
            P(),
            P(None, "chan"),
            P("chan"),
            P("chan"),
            P("section", "batch", None, "chan"),
        ),
        out_specs=(
            P("section", "batch", None, "chan"),
            P(None, "chan"),
            P(("section", "chan", "batch"), None),
        ),
        check_vma=False,
    )
```

profile of v0, /device:TPU:0, one launch (start us, length us, event | category | flops | bytes accessed | tf_op | source)
XLA Modules:
  0.0 1626.8 jit_solution(17548925114195281636)
XLA Ops:
  7.2 0.0 all-gather.3.cloned.1.call-start
  7.2 1.0 copy-done
  8.2 3.5 convert_reduce_fusion
  11.7 331.1 %all-reduce.1 = (f32[2048]{0:T(1024)S(1)}, f32[2048]{0:T(1024)S(1)}) all-reduce(f32[2048]{0:T(1024)S(1)} %get-tuple-element.16, f32[2048]{0:T(1024)S(1)} %get-tuple-element.15), channel_id=1, replica_groups=mesh['section'=2,'chan'=8,'batch'=8] {'chan','batch'}, use_global_device_ids=true, to_apply=%region_3.0 | all-reduce | flops 4096 | bytes 32768 | tf_op jit(solution)/shard_map/psum | solution.py:26
  342.8 1.7 fusion.12
  344.5 0.0 reduce-scatter.5.cloned.1.call-start
  344.6 103.3 %all-gather.3.cloned.1.call-done = bf16[2048,2048]{1,0:T(8,128)(2,1)} async-done(((bf16[256,2048]{1,0:T(8,128)(2,1)}), bf16[2048,2048]{1,0:T(8,128)(2,1)}) %all-gather.3.cloned.1.call-update) | async-done | bytes 8388624 | tf_op jit(solution)/shard_map/all_gather | solution.py:32
  447.8 14.5 fusion.34
  462.3 14.4 all-reduce.3
  476.8 7.5 fusion.33
  484.3 12.9 all-reduce.2
  497.2 9.8 multiply_convert_fusion
  507.0 2.0 copy-done.1
  509.0 11.1 convolution_convert_fusion
  520.1 0.0 all-reduce.6.cloned.1.call-start
  520.1 14.0 convolution_convert_fusion.1
  534.1 0.0 reduce-scatter.7.cloned.1.call-start
  534.2 96.1 %reduce-scatter.5.cloned.1.call-done = bf16[1,256,2048]{2,1,0:T(8,128)(2,1)} async-done(((bf16[8,256,2048]{2,1,0:T(8,128)(2,1)}), bf16[1,256,2048]{2,1,0:T(8,128)(2,1)}) %reduce-scatter.5.cloned.1.call-update) | async-done | bytes 1048592 | tf_op jit(solution)/shard_map/reduce_scatter | solution.py:53
  630.3 2.5 fusion.32
  632.8 325.9 %all-reduce = (f32[2048]{0:T(1024)S(1)}, f32[2048]{0:T(1024)S(1)}) all-reduce(f32[2048]{0:T(1024)S(1)} %get-tuple-element.14, f32[2048]{0:T(1024)S(1)} %get-tuple-element.13), channel_id=1, replica_groups=mesh['section'=2,'chan'=8,'batch'=8] {'chan','batch'}, use_global_device_ids=true, to_apply=%region_17.0 | all-reduce | flops 4096 | bytes 32768 | tf_op jit(solution)/shard_map/psum | solution.py:63
  958.7 6.9 convolution_bitcast_fusion
  965.6 9.1 copy.13
  974.8 6.6 convert_element_type.42
  981.5 638.8 %reduce-scatter.7.cloned.1.call-done = f32[8,2048]{1,0:T(8,128)} async-done(((f32[1024,2048]{1,0:T(8,128)}), f32[8,2048]{1,0:T(8,128)}) %reduce-scatter.7.cloned.1.call-update) | async-done | bytes 65552
  (22 shorter events, 0.2 us)
Async XLA Ops:
  7.2 1.0 copy-start
  7.2 335.6 %copy-start.2 = (f32[2048]{0:T(1024)S(1)}, f32[2048]{0:T(1024)}, u32[]{:S(2)}) copy-start(f32[2048]{0:T(1024)} %param.10) | copy-start | bytes 24580
  7.2 335.6 %copy-start.4 = (f32[2048]{0:T(1024)S(1)}, f32[2048]{0:T(1024)}, u32[]{:S(2)}) copy-start(f32[2048]{0:T(1024)} %param.11) | copy-start | bytes 24580
  7.2 440.6 %all-gather.3.cloned.1.call-start = ((), (), s32[]{:S(2)}) async-start(), calls=%async_computation.4 | async-start | bytes 9437184 | tf_op jit(solution)/shard_map/all_gather | solution.py:32
  344.5 132.3 %copy-start.3 = (f32[1024]{0:T(1024)S(1)}, f32[1024]{0:T(1024)}, u32[]{:S(2)}) copy-start(f32[1024]{0:T(1024)} %param.13) | copy-start | bytes 12292
  344.5 132.3 %copy-start.5 = (f32[1024]{0:T(1024)S(1)}, f32[1024]{0:T(1024)}, u32[]{:S(2)}) copy-start(f32[1024]{0:T(1024)} %param.14) | copy-start | bytes 12292
  344.5 285.8 %reduce-scatter.5.cloned.1.call-start = ((), (), s32[]{:S(2)}) async-start(), calls=%async_computation.3 | async-start | bytes 9437184 | tf_op jit(solution)/shard_map/reduce_scatter | solution.py:53
  497.2 11.8 copy-start.6
  507.0 2.0 copy-start.1
  520.1 454.7 %all-reduce.6.cloned.1.call-start = ((), (), s32[]{:S(2)}) async-start(), calls=%async_computation.2 | async-start | bytes 8388608 | tf_op jit(solution)/shard_map/psum | solution.py:50
  534.1 1086.1 %reduce-scatter.7.cloned.1.call-start = ((), (), s32[]{:S(2)}) async-start(), calls=%async_computation.5 | async-start | bytes 8454144
Sparse Core Ops, SparseCore 0:
  344.6 103.1 all-gather.2
  520.2 110.0 reduce-scatter.4
  632.8 127.4 all-reduce.5
  974.9 645.2 reduce-scatter.6
where the time goes:
time: 1630 us
  waiting for transfers between devices  838 us (51%)
  blocking collectives  684 us (42%)
  matrix products  49.9 us (3%)
  other arithmetic  28.2 us (2%)
    unnamed x5, waiting for transfers between devices  639 us
    psum x1, blocking collectives, body(): lax.psum((jnp.sum(raw_f, 0), jnp.sum(raw_f * raw_f, 0)), ('chan', 'batch'))  331 us
    psum x1, blocking collectives, body(): lax.psum((jnp.sum(grad_pre, 0), jnp.sum(grad_pre * normed_e, 0)), ('chan'...  326 us
    all_gather x1, waiting for transfers between devices, body(): act_full = lax.all_gather(act_local, 'chan', axis=0, tiled=True)  103 us
    reduce_scatter x1, waiting for transfers between devices, body(): lax.psum_scatter(jnp.einsum('ipl,al->ipa', piece, w_late, preferred_eleme...  96.1 us
  transfers between devices with their start and end apart: 4, of which 3 were waited for; matrix products, arithmetic and copies ran while one was open for 2% of the time, Pallas kernels for 0%

commit v1 on v0

v1 whole, which is shorter than its diff:
```python
import jax
import jax.numpy as jnp
from jax import lax
from jax.sharding import PartitionSpec as P

BF = jnp.bfloat16
F32 = jnp.float32


def shift(value, axis, step):
    return lax.ppermute(
        value, axis, [(i, ((i // 2 - step) % 4) * 2 + i % 2) for i in range(8)]
    )


def swap(value, axis):
    size = 2 if axis == "section" else 8
    return lax.ppermute(value, axis, [(i, i ^ 1) for i in range(size)])


def sum_pair(value, axis):
    return value + swap(value, axis)


def sum_ring(value, axis):
    one, two, three = (shift(value, axis, step) for step in (1, 2, 3))
    return (value + two) + (one + three)


def sum_batch(value):
    return sum_ring(sum_pair(value, "batch"), "batch")


def sum_all(value):
    return sum_pair(sum_ring(sum_batch(value), "chan"), "chan")


def block_of(value, index, rows):
    return lax.dynamic_slice_in_dim(value, index * rows, rows, 0)


def scatter_pair(value, axis, mine):
    rows = value.shape[0] // 2
    other = swap(block_of(value, 1 - mine, rows), axis)
    return block_of(value, mine, rows).astype(F32) + other.astype(F32)


def scatter_ring(value, axis, mine):
    rows = value.shape[0] // 4
    parts = [
        shift(block_of(value, (mine - step) % 4, rows), axis, step).astype(F32)
        for step in (1, 2, 3)
    ]
    return (block_of(value, mine, rows).astype(F32) + parts[1]) + (parts[0] + parts[2])


def gather_ring(value, axis, mine):
    rows = value.shape[0]
    full = jnp.zeros((4 * rows,) + value.shape[1:], value.dtype)
    full = lax.dynamic_update_slice_in_dim(full, value, mine * rows, 0)
    for step in (1, 2, 3):
        full = lax.dynamic_update_slice_in_dim(
            full, shift(value, axis, step), (mine + step) % 4 * rows, 0
        )
    return full


def gather_pair(value, axis, mine):
    other = swap(value, axis)
    first = jnp.where(mine == 0, value, other)
    second = jnp.where(mine == 0, other, value)
    return jnp.concatenate([first, second], 0)


def fwd_block(rows, w_early, w_late, scale, offset):
    raw = jnp.dot(rows, w_early, preferred_element_type=F32)
    pre = raw * scale + offset
    sig = jax.nn.sigmoid(pre)
    act = pre * sig
    slope = (sig + act * (1.0 - sig)).astype(BF)
    act = act.astype(BF)
    late = jnp.dot(act, w_late, preferred_element_type=F32)
    return raw.astype(BF), act, slope, late, jnp.stack([jnp.sum(late, 0), jnp.sum(late * late, 0)])


def body(images, w_early, gain_early, bias_early, w_late, gain_late, bias_late, cotangent):
    width_in, width_mid = w_early.shape
    width_out = w_late.shape[1]
    pixels = images.shape[3]
    own = images.reshape(pixels, width_in)
    chan = lax.axis_index("chan")
    batch = lax.axis_index("batch")
    x_pos, z_pos = chan // 2, chan % 2
    y_pos, core = batch // 2, batch % 2
    count = float(pixels * 64)

    raw_own = jnp.dot(own, w_early, preferred_element_type=F32).astype(BF).astype(F32)
    sums_e = sum_all(jnp.stack([jnp.sum(raw_own, 0), jnp.sum(raw_own * raw_own, 0)]))
    mean_e = sums_e[0] / count
    rstd_e = lax.rsqrt(sums_e[1] / count - mean_e * mean_e + 1e-05)
    scale_e = rstd_e * gain_early
    offset_e = bias_early - mean_e * scale_e

    half = pixels // 2
    right = shift(own, "chan", 1)
    left = shift(own, "chan", 3)
    deep = swap(own, "chan")
    far = jnp.concatenate([shift(right[:half], "chan", 1), shift(left[half:], "chan", 3)], 0)
    deep_right = shift(deep, "chan", 1)
    deep_left = shift(deep, "chan", 3)
    deep_far = swap(far, "chan")
    order = [
        ((x_pos + dx) % 4) * 2 + (z_pos ^ dz)
        for dx, dz in ((0, 0), (1, 0), (3, 0), (0, 1), (2, 0), (1, 1), (3, 1), (2, 1))
    ]
    groups = [
        jnp.concatenate([own, right, left, deep], 0),
        jnp.concatenate([far, deep_right, deep_left], 0),
        deep_far,
    ]
    done = [fwd_block(rows, w_early, w_late, scale_e, offset_e) for rows in groups]
    rows_all = jnp.concatenate(groups, 0)
    raw, act, slope, late = (jnp.concatenate([d[k] for d in done], 0) for k in range(4))
    sums_l = sum_batch(done[0][4] + done[1][4] + done[2][4])
    mean_l = sums_l[0] / count
    rstd_l = lax.rsqrt(sums_l[1] / count - mean_l * mean_l + 1e-05)

    cot = cotangent.reshape(8, pixels, width_out)
    cot = jnp.concatenate([lax.dynamic_index_in_dim(cot, j, 0, False) for j in order], 0)
    normed_l = (late - mean_l) * rstd_l
    pre_l = normed_l * gain_late + bias_late
    sig_l = jax.nn.sigmoid(pre_l)
    out_l = pre_l * sig_l
    grad_y = cot.astype(F32) * (sig_l + out_l * (1.0 - sig_l))
    back = sum_batch(jnp.stack([jnp.sum(grad_y, 0), jnp.sum(grad_y * normed_l, 0)])) / count
    grad_h = (gain_late * rstd_l * (grad_y - back[0] - normed_l * back[1])).astype(BF)
    out_rel = out_l.astype(BF).reshape(8, pixels, width_out)
    late_out = jnp.zeros_like(out_rel)
    for k, j in enumerate(order):
        late_out = lax.dynamic_update_slice_in_dim(late_out, out_rel[k : k + 1], j, 0)
    late_out = late_out.reshape(cotangent.shape)

    pieces = []
    for cols in jnp.split(grad_h, 2, axis=1):
        part = lax.dot_general(
            act, cols, (((0,), (0,)), ((), ())), preferred_element_type=F32
        ).astype(BF)
        part = scatter_pair(part, "batch", core).astype(BF)
        part = scatter_ring(part, "batch", y_pos).astype(BF)
        part = sum_pair(part.astype(F32).astype(BF), "section")
        part = gather_ring(part, "batch", y_pos)
        pieces.append(gather_pair(part, "batch", core))
    grad_late = jnp.concatenate(pieces, 1).astype(F32)

    rows_cut = rows_all.reshape(-1, 2, 4, 2, 4, 2, 8)
    rows_cut = jnp.transpose(rows_cut, (0, 5, 2, 3, 4, 1, 6)).reshape(-1, width_in)
    parts, sums_g = [], []
    step = width_mid // 4
    for k in range(4):
        cut = slice(k * step, (k + 1) * step)
        grad_act = lax.dot_general(
            grad_h, w_late[cut], (((1,), (1,)), ((), ())), preferred_element_type=F32
        )
        grad_pre = grad_act * slope[:, cut].astype(F32)
        sums_g.append(
            jnp.stack([jnp.sum(grad_pre, 0), jnp.sum(grad_pre * raw[:, cut].astype(F32), 0)])
        )
        term = lax.dot_general(
            rows_cut,
            grad_pre.astype(BF),
            (((0,), (0,)), ((), ())),
            preferred_element_type=F32,
        ).astype(BF)
        term = scatter_pair(term, "batch", core).astype(BF)
        parts.append(scatter_ring(term, "chan", x_pos).astype(BF))
    sums_g = sum_all(jnp.concatenate(sums_g, 1)) / count
    back_one = sums_g[0]
    back_two = rstd_e * (sums_g[1] - mean_e * sums_g[0])
    grad = scatter_pair(jnp.concatenate(parts, 1), "chan", z_pos)

    here = rows_cut.reshape(-1, 2, 8, 64)
    here = lax.dynamic_index_in_dim(here, chan, 2, False).reshape(-1, 128)
    cross = lax.dot_general(here, raw, (((0,), (0,)), ((), ())), preferred_element_type=F32)
    colsum = jnp.sum(here.astype(F32), 0)
    cross = jnp.concatenate([cross, jnp.broadcast_to(colsum[:, None], (128, 128))], 1)
    cross = scatter_pair(cross, "batch", core)
    colsum = cross[:, width_mid:][:, :1]
    cross = rstd_e * (cross[:, :width_mid] - colsum * mean_e)
    grad = scale_e * (grad - colsum * back_one - cross * back_two)
    grad = scatter_ring(grad, "batch", y_pos)
    section = lax.axis_index("section")
    grad_early = scatter_pair(grad, "section", section)
    return (late_out, grad_late, grad_early)


def solution(mesh):
    return jax.shard_map(
        body,
        mesh=mesh,
        in_specs=(
            P("section", "batch", "chan", None, None),
            P(),
            P(),
            P(),
            P(None, "chan"),
            P("chan"),
            P("chan"),
            P("section", "batch", None, "chan"),
        ),
        out_specs=(
            P("section", "batch", None, "chan"),
            P(None, "chan"),
            P(("section", "chan", "batch"), None),
        ),
        check_vma=False,
    )
```

time: 1630 us -> 355 us (0.22)
  waiting for transfers between devices: 838 us -> 92.1 us
  blocking collectives: 684 us -> 0 us
  starting transfers between devices: 0.16 us -> 82.3 us
  matrix products: 49.9 us -> 95.4 us
  local copies, waits for them, and re-layouts: 12.1 us -> 33.3 us
    psum x4 -> x0, blocking collectives: 684 us -> none  [the longest x1 331 us: body(): lax.psum((jnp.sum(raw_f, 0), jnp.sum(raw_f * raw_f, 0)), ('chan', 'batch'))]
    unnamed x5 -> x0, waiting for transfers between devices: 639 us -> none
    all_gather x1 -> x0, waiting for transfers between devices: 103 us -> none  [body(): act_full = lax.all_gather(act_local, 'chan', axis=0, tiled=True)]
    reduce_scatter x1 -> x0, waiting for transfers between devices: 96.1 us -> none  [body(): lax.psum_scatter(jnp.einsum('ipl,al->ipa', piece, w_late, preferred_eleme...]
    ppermute x0 -> x72, waiting for transfers between devices: none -> 92.1 us  [the longest x51 77.2 us: shift(): lax.ppermute(value, axis, [(i, (i // 2 - step) % 4 * 2 + i % 2) for i in...]
    ppermute x0 -> x72, starting transfers between devices: none -> 82.3 us  [the longest x51 60.7 us: shift(): lax.ppermute(value, axis, [(i, (i // 2 - step) % 4 * 2 + i % 2) for i in...]
    dot_general x5 -> x18, matrix products: 49.9 us -> 95.4 us  [the longest x4 28.7 us: body(): lax.dot_general(grad_h, w_late[cut], (((1,), (1,)), ((), ())), preferred_...]
  transfers between devices with their start and end apart: 4 -> 72, of which waited for: 3 -> 35; matrix products, arithmetic and copies ran while one was open for 2% -> 41% of each run, Pallas kernels for 0% -> 0%
where the time goes in v1:
time: 355 us; the launch traced here: 349 us
  matrix products  95.4 us (27%)
  waiting for transfers between devices  92.1 us (26%)
  starting transfers between devices  82.3 us (23%)
  other arithmetic  43.7 us (12%)
  local copies, waits for them, and re-layouts  33.3 us (9%)
    ppermute x51, waiting for transfers between devices, shift(): lax.ppermute(value, axis, [(i, (i // 2 - step) % 4 * 2 + i % 2) for i in...  77.2 us
    ppermute x51, starting transfers between devices, shift(): lax.ppermute(value, axis, [(i, (i // 2 - step) % 4 * 2 + i % 2) for i in...  60.7 us
    dot_general x4, matrix products, body(): lax.dot_general(grad_h, w_late[cut], (((1,), (1,)), ((), ())), preferred_...  28.7 us
    ppermute x21, starting transfers between devices, swap(): return lax.ppermute(value, axis, [(i, i ^ 1) for i in range(size)])  21.7 us
    dot_general x3, matrix products, fwd_block(): raw = jnp.dot(rows, w_early, preferred_element_type=F32)  20.8 us
    unnamed x74, local copies, waits for them, and re-layouts  20.5 us
    convert_element_type x1, other arithmetic, body(): grad_late = jnp.concatenate(pieces, 1).astype(F32)  17.6 us
    ppermute x21, waiting for transfers between devices, swap(): return lax.ppermute(value, axis, [(i, i ^ 1) for i in range(size)])  14.9 us
  transfers between devices with their start and end apart: 72, of which 35 were waited for; matrix products, arithmetic and copies ran while one was open for 41% of the time, Pallas kernels for 0%

profile of v1, /device:TPU:0, one launch (start us, length us, event | category | flops | bytes accessed | tf_op | source)
XLA Modules:
  0.0 348.9 jit_solution(3802349206517171761)
XLA Ops:
  34.5 3.9 %collective-permute-start.2 = (bf16[256,1024]{0,1:T(8,128)(2,1)S(1)}, bf16[256,1024]{0,1:T(8,128)(2,1)S(1)}, u32[]{:S(2)}, u32[]{:S(2)}) collective-permute-start(bf16[256,1024]{0,1:T(8,128)(2,1)S(1)} %bitcast.128), channel_id=1, source_target_pairs={{0,8},{8,0},{16,24},{24,16},{32,40},{40,32},{48,56},{56,48},{1,9},... | collective-permute-start | bytes 1572872 | tf_op jit(solution)/shard_map/ppermute | solution.py:18
  42.5 6.1 %collective-permute-done.10 = f32[2,2048]{1,0:T(2,128)S(1)} collective-permute-done((f32[2,2048]{1,0:T(2,128)S(1)}, f32[2,2048]{1,0:T(2,128)S(1)}, u32[]{:S(2)}, u32[]{:S(2)}) %collective-permute-start.10) | collective-permute-done | bytes 16416 | tf_op jit(solution)/shard_map/ppermute | solution.py:18
  52.0 10.1 %add_convert_fusion = (bf16[1024,2048]{1,0:T(8,128)(2,1)S(1)}, bf16[1024,2048]{1,0:T(8,128)(2,1)S(1)}, bf16[1024,2048]{1,0:T(8,128)(2,1)S(1)}) fusion(f32[2048]{0:T(1024)S(1)} %get-tuple-element.39, f32[2048]{0:T(1024)S(1)} %get-tuple-element.40, bf16[1024,2048]{1,0:T(8,128)(2,1)} %param.9, bf16[256,1024]{0,1:T(8,128)(2,1)S(1)} %collective-permute-done.2, ...), kind=kOutput, calls=%fused_computation.5 | convolution fusion | flops 4328521728 | bytes 18890752 | tf_op jit(solution)/shard_map/dot_general | solution.py:76
  64.1 6.1 %fusion.82 = (f32[1024]{0:T(1024)S(1)}, f32[1024]{0:T(1024)S(1)}, f32[1024,1024]{1,0:T(8,128)}) fusion(bf16[1024,2048]{1,0:T(8,128)(2,1)S(1)} %get-tuple-element.42, bf16[2048,1024]{1,0:T(8,128)(2,1)S(1)} %copy-done.19), kind=kOutput, calls=%fused_computation.217 | convolution fusion | flops 4298110976 | bytes 12591104 | tf_op jit(solution)/shard_map/dot_general | solution.py:82
  77.6 4.1 %collective-permute-done.13 = bf16[256,1024]{0,1:T(8,128)(2,1)S(1)} collective-permute-done((bf16[256,1024]{0,1:T(8,128)(2,1)S(1)}, bf16[256,1024]{0,1:T(8,128)(2,1)S(1)}, u32[]{:S(2)}, u32[]{:S(2)}) %collective-permute-start.13) | collective-permute-done | bytes 524320 | tf_op jit(solution)/shard_map/ppermute | solution.py:11
  85.3 7.5 %add_convert_fusion.1 = (bf16[768,2048]{1,0:T(8,128)(2,1)S(1)}, bf16[768,2048]{1,0:T(8,128)(2,1)}, bf16[768,2048]{1,0:T(8,128)(2,1)}) fusion(f32[2048]{0:T(1024)S(1)} %get-tuple-element.39, f32[2048]{0:T(1024)S(1)} %get-tuple-element.40, bf16[1024,2048]{1,0:T(8,128)(2,1)S(1)} %copy-done.18, bf16[256,1024]{0,1:T(8,128)(2,1)S(1)} %collective-permute-done.14, ...), kind=kOutput, calls=%fused_computation.17 | convolution fusion | flops 3246391296 | bytes 15220736 | tf_op jit(solution)/shard_map/dot_general | solution.py:76
  92.8 5.4 %fusion.83 = (f32[1024]{0:T(1024)S(1)}, f32[1024]{0:T(1024)S(1)}, f32[768,1024]{1,0:T(8,128)S(1)}) fusion(bf16[768,2048]{1,0:T(8,128)(2,1)} %get-tuple-element.46, bf16[2048,1024]{1,0:T(8,128)(2,1)S(1)} %copy-done.19), kind=kOutput, calls=%fused_computation.218 | convolution fusion | flops 3223582720 | bytes 10493952 | tf_op jit(solution)/shard_map/dot_general | solution.py:82
  106.5 7.1 %pad_maximum_fusion.1 = (bf16[2048,2048]{1,0:T(8,128)(2,1)}, bf16[2048,2048]{1,0:T(8,128)(2,1)S(1)}) fusion(bf16[256,2048]{1,0:T(8,128)(2,1)} %get-tuple-element.48, bf16[768,2048]{1,0:T(8,128)(2,1)S(1)} %get-tuple-element.45, bf16[1024,2048]{1,0:T(8,128)(2,1)S(1)} %get-tuple-element.41, bf16[256,2048]{1,0:T(8,128)(2,1)} %get-tuple-element.50, ...), kind=kLoop, calls=%fused_computation.3 | loop fusion | flops 50331648 | bytes 33554432 | tf_op jit(solution)/shard_map/concatenate | solution.py:123
  125.1 7.1 %fusion.81 = (f32[1024]{0:T(1024)S(1)}, f32[1024]{0:T(1024)S(1)}, f32[2048,1024]{1,0:T(8,128)S(1)}, bf16[2048,1024]{1,0:T(8,128)(2,1)S(1)}) fusion(f32[1024]{0:T(1024)S(1)} %bitcast.146, f32[1024]{0:T(1024)S(1)} %bitcast.155, f32[256,1024]{1,0:T(8,128)} %get-tuple-element.88, f32[768,1024]{1,0:T(8,128)S(1)} %get-tuple-element.86, ...), kind=kLoop, calls=%fused_computation.216 | loop fusion | flops 39843840 | bytes 25190400 | tf_op jit(solution)/shard_map/reduce_sum | solution.py:135
  147.7 5.2 %multiply_convert_fusion = bf16[2048,1024]{1,0:T(8,128)(2,1)} fusion(f32[2048,1024]{1,0:T(8,128)S(1)} %get-tuple-element.38, f32[1024]{0:T(1024)S(1)} %bitcast.162, f32[1024]{0:T(1024)S(1)} %bitcast.161, f32[1024]{0:T(1024)S(1)} %mul.358, f32[1024]{0:T(1024)S(1)} %bitcast.148, f32[1024]{0:T(1024)S(1)} %bitcast.156, f32[256,1024]{1,0:T(8,128)S(1)} %copy-done.9, ...), kind=kLoop, calls=%fused_computation.6 | loop fusion | flops 18874368 | bytes 20992000 | tf_op jit(solution)/shard_map/convert_element_type | solution.py:136
  152.9 5.9 %convert_multiply_fusion.2 = f32[2048,512]{1,0:T(8,128)S(1)} fusion(bf16[2048,1024]{1,0:T(8,128)(2,1)} %multiply_convert_fusion, bf16[2048,2048]{1,0:T(8,128)(2,1)} %get-tuple-element.90, bf16[2048,1024]{1,0:T(8,128)(2,1)} %param.12), kind=kOutput, calls=%fused_computation.29 | convolution fusion | flops 2149580800 | bytes 11534336 | tf_op jit(solution)/shard_map/dot_general | solution.py:161
  158.9 5.7 %convert_multiply_fusion.1 = f32[2048,512]{1,0:T(8,128)S(1)} fusion(bf16[2048,1024]{1,0:T(8,128)(2,1)S(1)} %copy-done.7, bf16[2048,2048]{1,0:T(8,128)(2,1)} %get-tuple-element.90, bf16[2048,1024]{1,0:T(8,128)(2,1)S(1)} %copy-done.20), kind=kOutput, calls=%fused_computation.28 | convolution fusion | flops 2149580800 | bytes 11534336 | tf_op jit(solution)/shard_map/dot_general | solution.py:161
  164.6 4.4 %convert_multiply_fusion = f32[2048,512]{1,0:T(8,128)} fusion(bf16[2048,1024]{1,0:T(8,128)(2,1)S(1)} %copy-done.7, bf16[2048,2048]{1,0:T(8,128)(2,1)S(1)} %bitcast.117, bf16[2048,1024]{1,0:T(8,128)(2,1)S(1)} %copy-done.20), kind=kOutput, calls=%fused_computation.27 | convolution fusion | flops 2149580800 | bytes 11534336 | tf_op jit(solution)/shard_map/dot_general | solution.py:161
  173.8 12.6 %multiply_reduce_fusion.4 = (f32[512]{0:T(512)S(1)}, f32[512]{0:T(512)S(1)}, f32[512]{0:T(512)S(1)}, f32[512]{0:T(512)S(1)}, f32[512]{0:T(512)S(1)}, /*index=5*/...) fusion(bf16[2048,2048]{1,0:T(8,128)(2,1)} %copy-done, ...), kind=kOutput, calls=%fused_computation.26 | convolution fusion | flops 2167402496 | bytes 30425088 | tf_op jit(solution)/shard_map/dot_general | solution.py:161
  186.5 4.7 %fusion.49 = bf16[1024,512]{1,0:T(8,128)(2,1)S(1)} fusion(bf16[2048,1024]{0,1:T(8,128)(2,1)S(1)} %bitcast.122, f32[2048,512]{1,0:T(8,128)} %convert_multiply_fusion), kind=kOutput, calls=%fused_computation.79 | convolution fusion | flops 2149056512 | bytes 9437184 | tf_op jit(solution)/shard_map/dot_general | solution.py:168
  191.2 6.9 %fusion.9 = bf16[2048,512]{1,0:T(8,128)(2,1)S(1)} fusion(bf16[256,2048]{1,0:T(8,128)(2,1)S(1)} %copy-done.22, bf16[768,2048]{1,0:T(8,128)(2,1)} %get-tuple-element.46, bf16[1024,2048]{1,0:T(8,128)(2,1)} %copy-done.26, bf16[2048,1024]{1,0:T(8,128)(2,1)S(1)} %copy-done.8), kind=kOutput, calls=%fused_computation.35 | convolution fusion | flops 4321181696 | bytes 12582912 | tf_op jit(solution)/shard_map/dot_general | solution.py:145
  198.1 7.0 %fusion.10 = bf16[2048,512]{1,0:T(8,128)(2,1)S(1)} fusion(bf16[256,2048]{1,0:T(8,128)(2,1)S(1)} %copy-done.22, bf16[768,2048]{1,0:T(8,128)(2,1)} %get-tuple-element.46, bf16[1024,2048]{1,0:T(8,128)(2,1)} %copy-done.26, bf16[2048,1024]{1,0:T(8,128)(2,1)S(1)} %copy-done.8), kind=kOutput, calls=%fused_computation.36 | convolution fusion | flops 4321181696 | bytes 12582912 | tf_op jit(solution)/shard_map/dot_general | solution.py:145
  231.9 4.4 %collective-permute-done.43 = bf16[128,512]{1,0:T(8,128)(2,1)S(1)} collective-permute-done((bf16[128,512]{1,0:T(8,128)(2,1)S(1)}, bf16[128,512]{1,0:T(8,128)(2,1)S(1)}, u32[]{:S(2)}, u32[]{:S(2)}) %collective-permute-start.43) | collective-permute-done | bytes 131104 | tf_op jit(solution)/shard_map/ppermute | solution.py:11
  239.6 4.6 %collective-permute-done.47 = bf16[128,512]{1,0:T(8,128)(2,1)S(1)} collective-permute-done((bf16[128,512]{1,0:T(8,128)(2,1)S(1)}, bf16[128,512]{1,0:T(8,128)(2,1)S(1)}, u32[]{:S(2)}, u32[]{:S(2)}) %collective-permute-start.47) | collective-permute-done | bytes 131104 | tf_op jit(solution)/shard_map/ppermute | solution.py:11
  258.4 4.4 %collective-permute-done.57 = bf16[128,512]{1,0:T(8,128)(2,1)S(1)} collective-permute-done((bf16[128,512]{1,0:T(8,128)(2,1)S(1)}, bf16[128,512]{1,0:T(8,128)(2,1)S(1)}, u32[]{:S(2)}, u32[]{:S(2)}) %collective-permute-start.57) | collective-permute-done | bytes 131104 | tf_op jit(solution)/shard_map/ppermute | solution.py:11
  278.5 4.0 %collective-permute-done.25 = bf16[256,512]{1,0:T(8,128)(2,1)S(1)} collective-permute-done((bf16[256,512]{1,0:T(8,128)(2,1)S(1)}, bf16[256,512]{1,0:T(8,128)(2,1)S(1)}, u32[]{:S(2)}, u32[]{:S(2)}) %collective-permute-start.25) | collective-permute-done | bytes 262176 | tf_op jit(solution)/shard_map/ppermute | solution.py:11
  301.6 5.0 %collective-permute-done.70 = f32[16,2048]{1,0:T(8,128)S(1)} collective-permute-done((f32[16,2048]{1,0:T(8,128)S(1)}, f32[16,2048]{1,0:T(8,128)S(1)}, u32[]{:S(2)}, u32[]{:S(2)}) %collective-permute-start.70) | collective-permute-done | bytes 131104 | tf_op jit(solution)/shard_map/ppermute | solution.py:11
  316.9 5.9 %collective-permute-done.31 = bf16[256,512]{1,0:T(8,128)(2,1)S(1)} collective-permute-done((bf16[256,512]{1,0:T(8,128)(2,1)S(1)}, bf16[256,512]{1,0:T(8,128)(2,1)S(1)}, u32[]{:S(2)}, u32[]{:S(2)}) %collective-permute-start.31) | collective-permute-done | bytes 262176 | tf_op jit(solution)/shard_map/ppermute | solution.py:11
  331.2 17.6 %maximum_convert_fusion = f32[2048,1024]{1,0:T(8,128)} fusion(bf16[1024,512]{1,0:T(8,128)(2,1)S(1)} %get-tuple-element.54, bf16[1024,512]{1,0:T(8,128)(2,1)S(1)} %get-tuple-element.53, bf16[1024,512]{1,0:T(8,128)(2,1)S(1)} %get-tuple-element.52, bf16[1024,512]{1,0:T(8,128)(2,1)S(1)} %get-tuple-element.51), kind=kLoop, calls=%fused_computation.22 | loop fusion | flops 16777216 | bytes 12582912 | tf_op jit(solution)/shard_map/convert_element_type | solution.py:153
  (303 shorter events, 191.2 us)
Async XLA Ops:
  1.9 46.9 %collective-permute-start = (bf16[256,1024]{0,1:T(8,128)(2,1)S(1)}, bf16[256,1024]{0,1:T(8,128)(2,1)S(1)}, u32[]{:S(2)}, u32[]{:S(2)}) collective-permute-start(bf16[256,1024]{0,1:T(8,128)(2,1)S(1)} %bitcast.125), channel_id=1, source_target_pairs={{0,48},{8,56},{16,0},{24,8},{32,16},{40,24},{48,32},{56,40},{1,49}... | collective-permute-start | bytes 1572872 | tf_op jit(solution)/shard_map/ppermute | solution.py:11
  4.8 46.6 %collective-permute-start.1 = (bf16[256,1024]{0,1:T(8,128)(2,1)S(1)}, bf16[256,1024]{0,1:T(8,128)(2,1)S(1)}, u32[]{:S(2)}, u32[]{:S(2)}) collective-permute-start(bf16[256,1024]{0,1:T(8,128)(2,1)S(1)} %bitcast.126), channel_id=1, source_target_pairs={{0,16},{8,24},{16,32},{24,40},{32,48},{40,56},{48,0},{56,8},{1,17}... | collective-permute-start | bytes 1572872 | tf_op jit(solution)/shard_map/ppermute | solution.py:11
  34.5 17.4 %collective-permute-start.2 = (bf16[256,1024]{0,1:T(8,128)(2,1)S(1)}, bf16[256,1024]{0,1:T(8,128)(2,1)S(1)}, u32[]{:S(2)}, u32[]{:S(2)}) collective-permute-start(bf16[256,1024]{0,1:T(8,128)(2,1)S(1)} %bitcast.128), channel_id=1, source_target_pairs={{0,8},{8,0},{16,24},{24,16},{32,40},{40,32},{48,56},{56,48},{1,9},... | collective-permute-start | bytes 1572872 | tf_op jit(solution)/shard_map/ppermute | solution.py:18
  48.8 25.0 %collective-permute-start.11 = (bf16[128,1024]{0,1:T(8,128)(2,1)S(1)}, bf16[128,1024]{0,1:T(8,128)(2,1)S(1)}, u32[]{:S(2)}, u32[]{:S(2)}) collective-permute-start(bf16[128,1024]{0,1:T(8,128)(2,1)S(1)} %slice.141), channel_id=1, source_target_pairs={{0,48},{8,56},{16,0},{24,8},{32,16},{40,24},{48,32},{56,40},{1,49}... | collective-permute-start | bytes 786440 | tf_op jit(solution)/shard_map/ppermute | solution.py:11
  51.4 22.4 %collective-permute-start.12 = (bf16[128,1024]{0,1:T(8,128)(2,1)S(1)}, bf16[128,1024]{0,1:T(8,128)(2,1)S(1)}, u32[]{:S(2)}, u32[]{:S(2)}) collective-permute-start(bf16[128,1024]{0,1:T(8,128)(2,1)S(1)} %slice.142), channel_id=1, source_target_pairs={{0,16},{8,24},{16,32},{24,40},{32,48},{40,56},{48,0},{56,8},{1,17}... | collective-permute-start | bytes 786440 | tf_op jit(solution)/shard_map/ppermute | solution.py:11
  70.3 11.4 %collective-permute-start.13 = (bf16[256,1024]{0,1:T(8,128)(2,1)S(1)}, bf16[256,1024]{0,1:T(8,128)(2,1)S(1)}, u32[]{:S(2)}, u32[]{:S(2)}) collective-permute-start(bf16[256,1024]{0,1:T(8,128)(2,1)S(1)} %collective-permute-done.2), channel_id=1, source_target_pairs={{0,48},{8,56},{16,0},{24,8},{32,16},{40,24},{48,32},{56,40},{1,49}... | collective-permute-start | bytes 1572872 | tf_op jit(solution)/shard_map/ppermute | solution.py:11
  73.6 11.6 %collective-permute-start.14 = (bf16[256,1024]{0,1:T(8,128)(2,1)S(1)}, bf16[256,1024]{0,1:T(8,128)(2,1)S(1)}, u32[]{:S(2)}, u32[]{:S(2)}) collective-permute-start(bf16[256,1024]{0,1:T(8,128)(2,1)S(1)} %collective-permute-done.2), channel_id=1, source_target_pairs={{0,16},{8,24},{16,32},{24,40},{32,48},{40,56},{48,0},{56,8},{1,17}... | collective-permute-start | bytes 1572872 | tf_op jit(solution)/shard_map/ppermute | solution.py:11
  73.9 24.3 %collective-permute-start.15 = (bf16[256,1024]{0,1:T(8,128)(2,1)S(1)}, bf16[256,1024]{0,1:T(8,128)(2,1)S(1)}, u32[]{:S(2)}, u32[]{:S(2)}) collective-permute-start(bf16[256,1024]{0,1:T(8,128)(2,1)S(1)} %pad_maximum_fusion.9), channel_id=1, source_target_pairs={{0,8},{8,0},{16,24},{24,16},{32,40},{40,32},{48,56},{56,48},{1,9},... | collective-permute-start | bytes 1572872 | tf_op jit(solution)/shard_map/ppermute | solution.py:18
  103.7 13.6 %collective-permute-start.16 = (f32[2,1024]{1,0:T(2,128)S(1)}, f32[2,1024]{1,0:T(2,128)S(1)}, u32[]{:S(2)}, u32[]{:S(2)}) collective-permute-start(f32[2,1024]{1,0:T(2,128)S(1)} %fusion.73), channel_id=1, source_target_pairs={{0,1},{1,0},{2,3},{3,2},{4,5},{5,4},{6,7},{7,6},{8,9},{9,8},{10,11... | collective-permute-start | bytes 24584 | tf_op jit(solution)/shard_map/ppermute | solution.py:18
  122.4 143.6 %collective-permute-start.59 = (f32[64,2176]{1,0:T(8,128)}, f32[64,2176]{1,0:T(8,128)}, u32[]{:S(2)}, u32[]{:S(2)}) collective-permute-start(f32[64,2176]{1,0:T(8,128)} %fusion.56), channel_id=1, source_target_pairs={{0,1},{1,0},{2,3},{3,2},{4,5},{5,4},{6,7},{7,6},{8,9},{9,8},{10,11... | collective-permute-start | bytes 1671176 | tf_op jit(solution)/shard_map/ppermute | solution.py:18
  207.7 20.1 %collective-permute-start.42 = (bf16[512,512]{1,0:T(8,128)(2,1)S(1)}, bf16[512,512]{1,0:T(8,128)(2,1)S(1)}, u32[]{:S(2)}, u32[]{:S(2)}) collective-permute-start(bf16[512,512]{1,0:T(8,128)(2,1)S(1)} %constant_dynamic-slice_fusion.21), channel_id=1, source_target_pairs={{0,1},{1,0},{2,3},{3,2},{4,5},{5,4},{6,7},{7,6},{8,9},{9,8},{10,11... | collective-permute-start | bytes 1572872 | tf_op jit(solution)/shard_map/ppermute | solution.py:18
  227.7 43.4 %collective-permute-start.24 = (bf16[1024,512]{1,0:T(8,128)(2,1)S(1)}, bf16[1024,512]{1,0:T(8,128)(2,1)S(1)}, u32[]{:S(2)}, u32[]{:S(2)}) collective-permute-start(bf16[1024,512]{1,0:T(8,128)(2,1)S(1)} %constant_dynamic-slice_fusion.29), channel_id=1, source_target_pairs={{0,1},{1,0},{2,3},{3,2},{4,5},{5,4},{6,7},{7,6},{8,9},{9,8},{10,11... | collective-permute-start | bytes 3145736 | tf_op jit(solution)/shard_map/ppermute | solution.py:18
  258.4 15.5 %collective-permute-start.33 = (bf16[1024,512]{1,0:T(8,128)(2,1)S(1)}, bf16[1024,512]{1,0:T(8,128)(2,1)S(1)}, u32[]{:S(2)}, u32[]{:S(2)}) collective-permute-start(bf16[1024,512]{1,0:T(8,128)(2,1)S(1)} %constant_dynamic-slice_fusion.25), channel_id=1, source_target_pairs={{0,1},{1,0},{2,3},{3,2},{4,5},{5,4},{6,7},{7,6},{8,9},{9,8},{10,11... | collective-permute-start | bytes 3145736 | tf_op jit(solution)/shard_map/ppermute | solution.py:18
  271.9 14.3 %collective-permute-start.26 = (bf16[256,512]{1,0:T(8,128)(2,1)S(1)}, bf16[256,512]{1,0:T(8,128)(2,1)S(1)}, u32[]{:S(2)}, u32[]{:S(2)}) collective-permute-start(bf16[256,512]{1,0:T(8,128)(2,1)S(1)} %get-tuple-element.57), channel_id=1, source_target_pairs={{0,6},{1,7},{2,0},{3,1},{4,2},{5,3},{6,4},{7,5},{8,14},{9,15},{10,... | collective-permute-start | bytes 786440 | tf_op jit(solution)/shard_map/ppermute | solution.py:11
  273.2 16.1 %collective-permute-start.27 = (bf16[256,512]{1,0:T(8,128)(2,1)S(1)}, bf16[256,512]{1,0:T(8,128)(2,1)S(1)}, u32[]{:S(2)}, u32[]{:S(2)}) collective-permute-start(bf16[256,512]{1,0:T(8,128)(2,1)S(1)} %get-tuple-element.56), channel_id=1, source_target_pairs={{0,2},{1,3},{2,4},{3,5},{4,6},{5,7},{6,0},{7,1},{8,10},{9,11},{10,... | collective-permute-start | bytes 786440 | tf_op jit(solution)/shard_map/ppermute | solution.py:11
  274.3 18.9 %collective-permute-start.34 = (bf16[256,512]{1,0:T(8,128)(2,1)S(1)}, bf16[256,512]{1,0:T(8,128)(2,1)S(1)}, u32[]{:S(2)}, u32[]{:S(2)}) collective-permute-start(bf16[256,512]{1,0:T(8,128)(2,1)S(1)} %get-tuple-element.58), channel_id=1, source_target_pairs={{0,4},{1,5},{2,6},{3,7},{4,0},{5,1},{6,2},{7,3},{8,12},{9,13},{10,... | collective-permute-start | bytes 786440 | tf_op jit(solution)/shard_map/ppermute | solution.py:11
  277.6 19.1 %collective-permute-start.35 = (bf16[256,512]{1,0:T(8,128)(2,1)S(1)}, bf16[256,512]{1,0:T(8,128)(2,1)S(1)}, u32[]{:S(2)}, u32[]{:S(2)}) collective-permute-start(bf16[256,512]{1,0:T(8,128)(2,1)S(1)} %get-tuple-element.60), channel_id=1, source_target_pairs={{0,6},{1,7},{2,0},{3,1},{4,2},{5,3},{6,4},{7,5},{8,14},{9,15},{10,... | collective-permute-start | bytes 786440 | tf_op jit(solution)/shard_map/ppermute | solution.py:11
  282.5 14.5 %collective-permute-start.36 = (bf16[256,512]{1,0:T(8,128)(2,1)S(1)}, bf16[256,512]{1,0:T(8,128)(2,1)S(1)}, u32[]{:S(2)}, u32[]{:S(2)}) collective-permute-start(bf16[256,512]{1,0:T(8,128)(2,1)S(1)} %get-tuple-element.59), channel_id=1, source_target_pairs={{0,2},{1,3},{2,4},{3,5},{4,6},{5,7},{6,0},{7,1},{8,10},{9,11},{10,... | collective-permute-start | bytes 786440 | tf_op jit(solution)/shard_map/ppermute | solution.py:11
  290.6 11.1 %collective-permute-start.68 = (f32[16,2048]{1,0:T(8,128)S(1)}, f32[16,2048]{1,0:T(8,128)S(1)}, u32[]{:S(2)}, u32[]{:S(2)}) collective-permute-start(f32[16,2048]{1,0:T(8,128)S(1)} %get-tuple-element.61), channel_id=1, source_target_pairs={{0,4},{1,5},{2,6},{3,7},{4,0},{5,1},{6,2},{7,3},{8,12},{9,13},{10,... | collective-permute-start | bytes 393224 | tf_op jit(solution)/shard_map/ppermute | solution.py:11
  298.6 15.5 %collective-permute-start.29 = (bf16[256,512]{1,0:T(8,128)(2,1)S(1)}, bf16[256,512]{1,0:T(8,128)(2,1)S(1)}, u32[]{:S(2)}, u32[]{:S(2)}) collective-permute-start(bf16[256,512]{1,0:T(8,128)(2,1)S(1)} %get-tuple-element.35), channel_id=1, source_target_pairs={{0,6},{1,7},{2,0},{3,1},{4,2},{5,3},{6,4},{7,5},{8,14},{9,15},{10,... | collective-permute-start | bytes 786440 | tf_op jit(solution)/shard_map/ppermute | solution.py:11
  306.7 16.1 %collective-permute-start.31 = (bf16[256,512]{1,0:T(8,128)(2,1)S(1)}, bf16[256,512]{1,0:T(8,128)(2,1)S(1)}, u32[]{:S(2)}, u32[]{:S(2)}) collective-permute-start(bf16[256,512]{1,0:T(8,128)(2,1)S(1)} %get-tuple-element.35), channel_id=1, source_target_pairs={{0,2},{1,3},{2,4},{3,5},{4,6},{5,7},{6,0},{7,1},{8,10},{9,11},{10,... | collective-permute-start | bytes 786440 | tf_op jit(solution)/shard_map/ppermute | solution.py:11
  307.1 15.8 %collective-permute-start.38 = (bf16[256,512]{1,0:T(8,128)(2,1)S(1)}, bf16[256,512]{1,0:T(8,128)(2,1)S(1)}, u32[]{:S(2)}, u32[]{:S(2)}) collective-permute-start(bf16[256,512]{1,0:T(8,128)(2,1)S(1)} %get-tuple-element.37), channel_id=1, source_target_pairs={{0,6},{1,7},{2,0},{3,1},{4,2},{5,3},{6,4},{7,5},{8,14},{9,15},{10,... | collective-permute-start | bytes 786440 | tf_op jit(solution)/shard_map/ppermute | solution.py:11
  310.3 12.7 %collective-permute-start.39 = (bf16[256,512]{1,0:T(8,128)(2,1)S(1)}, bf16[256,512]{1,0:T(8,128)(2,1)S(1)}, u32[]{:S(2)}, u32[]{:S(2)}) collective-permute-start(bf16[256,512]{1,0:T(8,128)(2,1)S(1)} %get-tuple-element.37), channel_id=1, source_target_pairs={{0,4},{1,5},{2,6},{3,7},{4,0},{5,1},{6,2},{7,3},{8,12},{9,13},{10,... | collective-permute-start | bytes 786440 | tf_op jit(solution)/shard_map/ppermute | solution.py:11
  314.1 11.5 %collective-permute-start.40 = (bf16[256,512]{1,0:T(8,128)(2,1)S(1)}, bf16[256,512]{1,0:T(8,128)(2,1)S(1)}, u32[]{:S(2)}, u32[]{:S(2)}) collective-permute-start(bf16[256,512]{1,0:T(8,128)(2,1)S(1)} %get-tuple-element.37), channel_id=1, source_target_pairs={{0,2},{1,3},{2,4},{3,5},{4,6},{5,7},{6,0},{7,1},{8,10},{9,11},{10,... | collective-permute-start | bytes 786440 | tf_op jit(solution)/shard_map/ppermute | solution.py:11
  (77 other events, 691.3 us)
